TPU v7x, 256 devices: a whole 4x4x8 slice. The times are simulated.
256 devices in a mesh: wide: 32 (over x, y, core), narrow: 8 (over z).
Axes of the slice: x: 4, y: 4, z: 8, core: 2. Of those that a mesh axis runs over, the one named last changes fastest.
Arguments:
- tokens: bfloat16 [16384, 4096], P('wide', 'narrow'), may hold values from -40 to 40
- norm_gain: float32 [4096], P('narrow'), may hold values from 0.5 to 5
- w_query: bfloat16 [4096, 4096], P(None, 'narrow'), may hold values from -0.09375 to 0.09375
- key_weight: bfloat16 [4096, 1024], P(None, 'narrow'), may hold values from -0.09375 to 0.09375
- value_weight: bfloat16 [4096, 1024], P(None, 'narrow'), may hold values from -0.09375 to 0.09375
- w_out: bfloat16 [4096, 4096], P('narrow'), may hold values from -0.09375 to 0.09375
- doc_lengths: int32 [64], replicated, may hold values from 1 to 8192, 16384 in all
Outputs:
- attended: bfloat16 [16384, 4096], P('wide', 'narrow')
Inputs may be any that keep to these rules, and one draw needn't show every extreme that they name: `doc_lengths`: the lengths sum to 16384; the longest is exactly 8192.
All inputs are finite; a program needn't handle non-finite values.
Results may differ from a plain program's by a relative error of at most 0.019.
The roundings to bfloat16 on the way count: a program that leaves them out, or rounds other values in their place, can miss the bound.
Values may be sent and summed in bfloat16 or wider, within the bound.
No kernel may reach another device: no remote copies, remote signals or barrier semaphores. Data moves between devices by JAX's collectives and lax.ppermute only.
A program may use at most 128 MiB of HBM per device.

v0:
```python
import math
import jax
import jax.numpy as jnp
from jax import lax
from jax.sharding import PartitionSpec as P

MODEL_WIDTH = 4096
HEAD_SIZE = 128
EPSILON = 1e-05
ROPE_BASE = 500000.0
NEGATIVE = -1e30


def doc_of(lengths, positions):
    starts = jnp.cumsum(lengths) - lengths
    return jnp.sum((starts[None, :] <= positions[:, None]).astype(jnp.int32), axis=1) - 1


def doc_info(lengths, positions):
    starts = jnp.cumsum(lengths) - lengths
    docs = doc_of(lengths, positions)
    onehot = docs[:, None] == jnp.arange(lengths.shape[0], dtype=jnp.int32)[None, :]
    first_tok = jnp.sum(jnp.where(onehot, starts[None, :], 0), axis=1)
    return (docs, positions - first_tok)


def apply_rotary(values, rotary_positions):
    half_width = values.shape[-1] // 2
    frequency = ROPE_BASE ** (-(jnp.arange(half_width, dtype=jnp.float32) * 2.0 / values.shape[-1]))
    angles = rotary_positions.astype(jnp.float32)[:, None] * frequency[None, :]
    cosine = jnp.cos(angles)[:, None, :]
    sine_part = jnp.sin(angles)[:, None, :]
    first_half = values[..., :half_width]
    second_half = values[..., half_width:]
    return jnp.concatenate(
        [
            first_half * cosine - second_half * sine_part,
            second_half * cosine + first_half * sine_part,
        ],
        axis=-1,
    )


def per_device(tokens, norm_gain, w_query, key_weight, value_weight, w_out, doc_lengths):
    tok_rows = tokens.shape[0]
    wide_index = lax.axis_index("wide")
    as_float = tokens.astype(jnp.float32)
    squares = lax.psum(jnp.sum(as_float * as_float, axis=1), "narrow")
    inverse = lax.rsqrt(squares / MODEL_WIDTH + EPSILON)
    normed = (as_float * inverse[:, None] * norm_gain[None, :]).astype(jnp.bfloat16)
    shard_piece = lax.all_gather(normed, "narrow", axis=1, tiled=True)
    query_raw, key_unrotated, value_projected = tuple(
        (
            jnp.dot(shard_piece, matrix, preferred_element_type=jnp.float32)
            for matrix in (w_query, key_weight, value_weight)
        )
    )
    positions = wide_index * tok_rows + jnp.arange(tok_rows, dtype=jnp.int32)
    own_doc, rotary_positions = doc_info(doc_lengths, positions)
    heads_local = w_query.shape[1] // HEAD_SIZE
    kv_local = key_weight.shape[1] // HEAD_SIZE
    heads_per_group = heads_local // kv_local
    queries_own = (
        apply_rotary(query_raw.reshape(tok_rows, heads_local, HEAD_SIZE), rotary_positions)
        .astype(jnp.bfloat16)
        .reshape(tok_rows, kv_local, heads_per_group, HEAD_SIZE)
    )
    rotated_keys = apply_rotary(
        key_unrotated.reshape(tok_rows, kv_local, HEAD_SIZE), rotary_positions
    ).astype(jnp.bfloat16)
    values_cast = value_projected.reshape(tok_rows, kv_local, HEAD_SIZE).astype(jnp.bfloat16)
    key_value = jnp.stack([rotated_keys, values_cast])
    score_scale = 1.0 / math.sqrt(HEAD_SIZE)
    last_pos = jnp.max(positions)
    first_doc = jnp.min(own_doc)

    def update(carried, key_tile, value_tile, key_pos, key_doc):
        run_max, run_sum, accum = carried
        scores = (
            jnp.einsum("rkgd,nkd->kgrn", queries_own, key_tile, preferred_element_type=jnp.float32)
            * score_scale
        )
        allowed = (key_doc[None, :] == own_doc[:, None]) & (key_pos[None, :] <= positions[:, None])
        masked = jnp.where(allowed, scores, NEGATIVE)
        new_max = jnp.maximum(run_max, jnp.max(masked, axis=-1))
        weights = jnp.where(allowed, jnp.exp(scores - new_max[..., None]), 0.0)
        factor = jnp.exp(run_max - new_max)
        run_sum = run_sum * factor + jnp.sum(weights, axis=-1)
        accum = accum * factor[..., None] + jnp.einsum(
            "kgrn,nkd->kgrd",
            weights.astype(jnp.bfloat16),
            value_tile,
            preferred_element_type=jnp.float32,
        )
        return (new_max, run_sum, accum)

    start_status = (
        jnp.full((kv_local, heads_per_group, tok_rows), NEGATIVE, jnp.float32),
        jnp.zeros((kv_local, heads_per_group, tok_rows), jnp.float32),
        jnp.zeros((kv_local, heads_per_group, tok_rows, HEAD_SIZE), jnp.float32),
    )
    pair = lax.all_gather(key_value, "wide", axis=1, tiled=True)
    count_keys = pair.shape[1]
    tile_width = math.gcd(count_keys, 512)
    tile_count = count_keys // tile_width

    def tile_step(tile_index, carried_in):
        offset = tile_index * tile_width
        key_tile = lax.dynamic_slice_in_dim(pair, offset, tile_width, 1)
        key_pos = offset + jnp.arange(tile_width, dtype=jnp.int32)
        key_doc = doc_of(doc_lengths, key_pos)
        needed = (key_pos[0] <= last_pos) & (key_doc[-1] >= first_doc)
        return lax.cond(
            needed,
            lambda status: update(status, key_tile[0], key_tile[1], key_pos, key_doc),
            lambda status: status,
            carried_in,
        )

    status_now = lax.fori_loop(0, tile_count, tile_step, start_status)
    run_max, run_sum, accum = status_now
    heads_out = (
        (accum / run_sum[..., None])
        .transpose(2, 0, 1, 3)
        .reshape(tok_rows, heads_local * HEAD_SIZE)
        .astype(jnp.bfloat16)
    )
    partial_out = jnp.dot(heads_out, w_out, preferred_element_type=jnp.float32)
    return lax.psum_scatter(
        partial_out.astype(jnp.bfloat16), "narrow", scatter_dimension=1, tiled=True
    )


def solution(mesh):
    in_specs = (
        P("wide", "narrow"),
        P("narrow"),
        P(None, "narrow"),
        P(None, "narrow"),
        P(None, "narrow"),
        P("narrow", None),
        P(),
    )
    out_specs = P("wide", "narrow")
    return jax.shard_map(
        per_device, mesh=mesh, in_specs=in_specs, out_specs=out_specs, check_vma=False
    )
```

profile of v0, /device:TPU:1, one launch (start us, length us, event | category | flops | bytes accessed | tf_op | source)
XLA Modules:
  0.0 502.4 jit_solution(14981264105822187456)
XLA Ops:
  6.5 1.3 fusion.25
  7.8 17.3 %psum.7 = f32[512]{0:T(512)S(1)} all-reduce(f32[512]{0:T(512)S(1)} %fusion.25), channel_id=1, replica_groups=mesh['wide'=32,'narrow'=8] {'narrow'}, use_global_device_ids=true, to_apply=%region_1.0 | all-reduce | flops 512 | bytes 4096 | tf_op jit(solution)/shard_map/psum | solution.py:48
  25.2 2.0 fusion.27
  27.3 0.8 copy.22
  28.3 0.7 sub.52
  29.1 0.7 broadcast_add_fusion.2
  29.9 54.0 %all-gather.3.cloned.1.call-done = bf16[512,4096]{1,0:T(8,128)(2,1)} async-done(((bf16[512,512]{1,0:T(8,128)(2,1)}), bf16[512,4096]{1,0:T(8,128)(2,1)}) %all-gather.3.cloned.1.call-update) | async-done | bytes 4194320 | tf_op jit(solution)/shard_map/all_gather | solution.py:51
  83.9 3.8 convolution_bitcast_fusion
  87.7 0.6 fusion.39
  88.3 1.5 fusion.24
  89.8 0.7 pad_maximum_fusion.1
  90.8 0.7 fusion.40
  91.5 1.7 multiply_cosine_fusion
  93.2 5.8 %fusion.43 = f32[512,512]{0,1:T(8,128)S(1)} fusion(bf16[512,4096]{1,0:T(8,128)(2,1)} %all-gather.3.cloned.1.call-done, bf16[4096,512]{1,0:T(8,128)(2,1)} %param.13), kind=kOutput, calls=%fused_computation.71 | convolution fusion | flops 2147483648 | bytes 9437184 | tf_op jit(solution)/shard_map/dot_general | solution.py:54
  99.1 0.9 fusion.42
  100.3 1.4 copy.31
  101.7 1.2 fusion.28
  103.2 51.1 %all-gather.5.cloned.1.call-done = bf16[2,16384,1,128]{1,3,2,0:T(8,128)(2,1)} async-done(((bf16[2,512,1,128]{1,3,2,0:T(8,128)(2,1)}), bf16[2,16384,1,128]{1,3,2,0:T(8,128)(2,1)}) %all-gather.5.cloned.1.call-update) | async-done | bytes 8388624 | tf_op jit(solution)/shard_map/all_gather | solution.py:102
  154.3 11.9 %copy.26 = bf16[2,16384,1,128]{3,1,2,0:T(8,128)(2,1)} copy(bf16[2,16384,1,128]{1,3,2,0:T(8,128)(2,1)} %all-gather.5.cloned.1.call-done) | data formatting | bytes 16777216
  166.3 134.6 %while.20 = (s32[]{:T(128)}, f32[1,4,512]{2,1,0:T(4,128)S(1)}, f32[1,4,512]{2,1,0:T(4,128)S(1)}, f32[1,4,512,128]{3,2,1,0:T(8,128)S(1)}, s32[]{:T(128)}, /*index...) while((s32[]{:T(128)}, f32[1,4,512]{2,1,0:T(4,128)S(1)}, ...), condition=%wide.region_13.14_spmd.clone, body=%wide.region_7.13_spmd.clone.sunk | while | flops 549821440 | bytes 33448608 | solution.py:120
  169.9 8.8 %conditional.3 = ((f32[1,4,512]{2,1,0:T(4,128)S(1)}, f32[1,4,512]{2,1,0:T(4,128)S(1)}, f32[1,4,512,128]{3,2,1,0:T(8,128)S(1)})) conditional(s32[]{:T(128)} %convert_element_type.114, (f32[1,4,512]{2,1,0:T(4,128)S(1)}, f32[1,4,512]{2,1,0:T(4,128)S(1)}, f32[1,4,512,128]{3,2,1,0:T(8,128)S(1)}) %tuple.65, (s32[512]{0:T(512)S(1)}, s32[512]{0:T(512)S(1)}, ...), branch_computations={%region_9.9_spmd, %region_10.12_spmd} | conditional | flops 549722624 | bytes 33435770 | solution.py:113
  170.2 3.7 fusion.2
  174.0 3.8 fusion.14
  177.8 0.9 fusion.6
  182.4 8.8 %conditional.3 = ((f32[1,4,512]{2,1,0:T(4,128)S(1)}, f32[1,4,512]{2,1,0:T(4,128)S(1)}, f32[1,4,512,128]{3,2,1,0:T(8,128)S(1)})) conditional(s32[]{:T(128)} %convert_element_type.114, (f32[1,4,512]{2,1,0:T(4,128)S(1)}, f32[1,4,512]{2,1,0:T(4,128)S(1)}, f32[1,4,512,128]{3,2,1,0:T(8,128)S(1)}) %tuple.65, (s32[512]{0:T(512)S(1)}, s32[512]{0:T(512)S(1)}, ...), branch_computations={%region_9.9_spmd, %region_10.12_spmd} | conditional | flops 549722624 | bytes 33435770 | solution.py:113
  182.7 3.7 fusion.2
  186.5 3.8 fusion.14
  190.3 0.9 fusion.6
  300.9 1.3 copy.27
  302.2 1.4 divide_convert_fusion
  303.6 6.5 %convolution_convert_fusion = bf16[512,4096]{1,0:T(8,128)(2,1)} fusion(bf16[512,512]{0,1:T(8,128)(2,1)S(1)} %bitcast.96, bf16[512,4096]{1,0:T(8,128)(2,1)} %param.16), kind=kOutput, calls=%fused_computation.30 | convolution fusion | flops 2149580800 | bytes 8912896 | tf_op jit(solution)/shard_map/dot_general | solution.py:128
  310.1 185.8 %reduce-scatter.2.cloned.1.call-done = bf16[512,512]{1,0:T(8,128)(2,1)} async-done(((bf16[512,4096]{1,0:T(8,128)(2,1)}), bf16[512,512]{1,0:T(8,128)(2,1)}) %reduce-scatter.2.cloned.1.call-update) | async-done | bytes 524304 | tf_op jit(solution)/shard_map/reduce_scatter | solution.py:129
  (261 shorter events, 39.1 us)
Async XLA Ops:
  6.5 77.4 %copy-start = (bf16[4096,128]{1,0:T(8,128)(2,1)S(1)}, bf16[4096,128]{1,0:T(8,128)(2,1)}, u32[]{:S(2)}) copy-start(bf16[4096,128]{1,0:T(8,128)(2,1)} %param.14) | copy-start | bytes 3145732
  6.5 77.4 %all-gather.3.cloned.1.call-start = ((), (), s32[]{:S(2)}) async-start(), calls=%async_computation.1 | async-start | bytes 4718592 | tf_op jit(solution)/shard_map/all_gather | solution.py:51
  27.2 61.1 %copy-start.3 = (bf16[4096,128]{1,0:T(8,128)(2,1)S(1)}, bf16[4096,128]{1,0:T(8,128)(2,1)}, u32[]{:S(2)}) copy-start(bf16[4096,128]{1,0:T(8,128)(2,1)} %param.15) | copy-start | bytes 3145732
  27.2 127.1 %all-gather.5.cloned.1.call-start = ((), (), s32[]{:S(2)}) async-start(), calls=%async_computation.2 | async-start | bytes 8650752 | tf_op jit(solution)/shard_map/all_gather | solution.py:102
  83.9 4.4 copy-start.2
  90.6 405.3 %reduce-scatter.2.cloned.1.call-start = ((), (), s32[]{:S(2)}) async-start(), calls=%async_computation.3 | async-start | bytes 4718592 | tf_op jit(solution)/shard_map/reduce_scatter | solution.py:129
  174.0 3.8 copy-start.1
  186.5 3.8 copy-start.1
Sparse Core Ops, SparseCore 0:
  27.3 56.5 all-gather.2
  90.7 63.5 all-gather.4
  310.2 185.6 reduce-scatter.1
where the time goes:
time: 505 us; the launch traced here: 502 us
  waiting for transfers between devices  291 us (58%)
  loops' own time  80.4 us (16%)
  local copies, waits for them, and re-layouts  50.1 us (10%)
  matrix products  32.8 us (6%)
  other arithmetic  17.4 us (3%)
  blocking collectives  17.3 us (3%)
  between operations  13.2 us (3%)
    reduce_scatter x1, waiting for transfers between devices, per_device(): lax.psum_scatter(partial_out.astype(jnp.bfloat16), 'narrow', scatter_dime...  186 us
    another operation x1, loops' own time, per_device(): status_now = lax.fori_loop(0, tile_count, tile_step, start_status)  79.9 us
    all_gather x1, waiting for transfers between devices, per_device(): shard_piece = lax.all_gather(normed, 'narrow', axis=1, tiled=True)  54 us
    all_gather x1, waiting for transfers between devices, per_device(): pair = lax.all_gather(key_value, 'wide', axis=1, tiled=True)  51.1 us
    slice x64, local copies, waits for them, and re-layouts, tile_step(): needed = (key_pos[0] <= last_pos) & (key_doc[-1] >= first_doc)  33.3 us
    psum x1, blocking collectives, per_device(): squares = lax.psum(jnp.sum(as_float * as_float, axis=1), 'narrow')  17.3 us
    unnamed x9, local copies, waits for them, and re-layouts  13.6 us
    dot_general x3, matrix products, per_device(): jnp.dot(shard_piece, matrix, preferred_element_type=jnp.float32)  11.2 us
  transfers between devices with their start and end apart: 3, of which 3 were waited for; matrix products, arithmetic and copies ran while one was open for 3% of the time, Pallas kernels for 0%

commit v1 on v0

--- a/solution.py
+++ b/solution.py
@@ -48,7 +48,9 @@
     squares = lax.psum(jnp.sum(as_float * as_float, axis=1), "narrow")
     inverse = lax.rsqrt(squares / MODEL_WIDTH + EPSILON)
     normed = (as_float * inverse[:, None] * norm_gain[None, :]).astype(jnp.bfloat16)
-    shard_piece = lax.all_gather(normed, "narrow", axis=1, tiled=True)
+    shard_piece = jnp.concatenate(
+        lax.all_to_all(jnp.stack([normed] * lax.axis_size("narrow")), "narrow", 0, 0), axis=1
+    )
     query_raw, key_unrotated, value_projected = tuple(
         (
             jnp.dot(shard_piece, matrix, preferred_element_type=jnp.float32)

time: 505 us -> 544 us (1.077)
  waiting for transfers between devices: 291 us -> 314 us
  local copies, waits for them, and re-layouts: 50.1 us -> 71.5 us
    all_to_all x0 -> x1, waiting for transfers between devices: none -> 89.5 us  [per_device(): lax.all_to_all(jnp.stack([normed] * lax.axis_size('narrow')), 'narrow', 0...]
    all_gather x1 -> x0, waiting for transfers between devices: 54 us -> none  [per_device(): shard_piece = lax.all_gather(normed, 'narrow', axis=1, tiled=True)]
    reshape x0 -> x3, local copies, waits for them, and re-layouts: none -> 16.7 us  [per_device(): jnp.concatenate(lax.all_to_all(jnp.stack([normed] * lax.axis_size('narrow...]
    all_gather x1, waiting for transfers between devices: 51.1 us -> 39.1 us  [per_device(): pair = lax.all_gather(key_value, 'wide', axis=1, tiled=True)]
    dot_general x0 -> x1, local copies, waits for them, and re-layouts: none -> 6.45 us  [per_device(): jnp.dot(shard_piece, matrix, preferred_element_type=jnp.float32)]
    unnamed x9 -> x10, local copies, waits for them, and re-layouts: 13.6 us -> 12.2 us
  transfers between devices with their start and end apart: 3 -> 3, of which waited for: 3 -> 3; matrix products, arithmetic and copies ran while one was open for 3% -> 5% of each run, Pallas kernels for 0% -> 0%
where the time goes in v1:
time: 544 us; the launch traced here: 541 us
  waiting for transfers between devices  314 us (58%)
  loops' own time  76.9 us (14%)
  local copies, waits for them, and re-layouts  71.5 us (13%)
  matrix products  30.6 us (6%)
  blocking collectives  17.3 us (3%)
  between operations  13.6 us (2%)
  other arithmetic  12.1 us (2%)
    reduce_scatter x1, waiting for transfers between devices, per_device(): lax.psum_scatter(partial_out.astype(jnp.bfloat16), 'narrow', scatter_dime...  186 us
    all_to_all x1, waiting for transfers between devices, per_device(): lax.all_to_all(jnp.stack([normed] * lax.axis_size('narrow')), 'narrow', 0...  89.5 us
    another operation x1, loops' own time, per_device(): status_now = lax.fori_loop(0, tile_count, tile_step, start_status)  76.3 us
    all_gather x1, waiting for transfers between devices, per_device(): pair = lax.all_gather(key_value, 'wide', axis=1, tiled=True)  39.1 us
    slice x64, local copies, waits for them, and re-layouts, tile_step(): needed = (key_pos[0] <= last_pos) & (key_doc[-1] >= first_doc)  33.3 us
    psum x1, blocking collectives, per_device(): squares = lax.psum(jnp.sum(as_float * as_float, axis=1), 'narrow')  17.3 us
    reshape x3, local copies, waits for them, and re-layouts, per_device(): jnp.concatenate(lax.all_to_all(jnp.stack([normed] * lax.axis_size('narrow...  16.7 us
    unnamed x10, local copies, waits for them, and re-layouts  12.2 us
  transfers between devices with their start and end apart: 3, of which 3 were waited for; matrix products, arithmetic and copies ran while one was open for 5% of the time, Pallas kernels for 0%

profile of v1, /device:TPU:1, one launch (start us, length us, event | category | flops | bytes accessed | tf_op | source)
XLA Modules:
  0.0 541.4 jit_solution(10826953725475290016)
XLA Ops:
  6.5 1.3 fusion.25
  7.8 17.3 %psum.7 = f32[512]{0:T(512)S(1)} all-reduce(f32[512]{0:T(512)S(1)} %fusion.25), channel_id=1, replica_groups=mesh['wide'=32,'narrow'=8] {'narrow'}, use_global_device_ids=true, to_apply=%region_1.0 | all-reduce | flops 512 | bytes 4096 | tf_op jit(solution)/shard_map/psum | solution.py:48
  25.2 1.2 fusion.27
  26.4 2.3 stack.6
  28.7 4.7 all-to-all-start
  33.9 0.6 broadcast_add_fusion.2
  34.7 89.5 %all-to-all-done = bf16[8,512,512]{2,1,0:T(8,128)(2,1)} async-done(((bf16[8,512,512]{2,1,0:T(8,128)(2,1)}), bf16[8,512,512]{2,1,0:T(8,128)(2,1)}, u32[]{:S(2)}, u32[]{:S(2)}) %all-to-all-start) | async-done | bytes 4194336 | tf_op jit(solution)/shard_map/all_to_all | solution.py:52
  124.1 2.8 copy.40
  127.0 1.5 convolution_bitcast_fusion
  128.5 1.5 fusion.24
  130.0 0.6 fusion.39
  130.6 0.7 pad_maximum_fusion.1
  131.6 0.6 fusion.40
  132.2 6.5 %copy.39 = bf16[512,4096]{1,0:T(8,128)(2,1)} copy(bf16[512,4096]{0,1:T(8,128)(2,1)} %bitcast.100) | data formatting | bytes 8388608 | tf_op jit(solution)/shard_map/dot_general | solution.py:56
  139.2 6.5 %copy.31 = bf16[512,8,512]{2,1,0:T(8,128)(2,1)} copy(bf16[512,8,512]{2,0,1:T(8,128)(2,1)} %bitcast.16) | data formatting | bytes 8388608 | tf_op jit(solution)/shard_map/reshape | solution.py:51
  145.7 7.4 %reshape.306 = bf16[512,4096,1]{1,0,2:T(8,128)(2,1)} reshape(bf16[512,8,512]{2,1,0:T(8,128)(2,1)} %copy.31) | data formatting | bytes 8388608 | tf_op jit(solution)/shard_map/reshape | solution.py:51
  153.1 5.9 %fusion.42 = f32[512,4,128]{0,2,1:T(8,128)S(1)} fusion(bf16[512,4096,1]{1,0,2:T(8,128)(2,1)} %reshape.306, bf16[4,128,4096]{2,1,0:T(8,128)(2,1)} %bitcast.101), kind=kOutput, calls=%fused_computation.70 | convolution fusion | flops 2147483648 | bytes 9437184 | tf_op jit(solution)/shard_map/dot_general | solution.py:56
  159.5 39.1 %all-gather.2.cloned.1.call-done = bf16[2,16384,1,128]{1,3,2,0:T(8,128)(2,1)} async-done(((bf16[2,512,1,128]{1,3,2,0:T(8,128)(2,1)}), bf16[2,16384,1,128]{1,3,2,0:T(8,128)(2,1)}) %all-gather.2.cloned.1.call-update) | async-done | bytes 8388624 | tf_op jit(solution)/shard_map/all_gather | solution.py:104
  198.6 11.9 %copy.34 = bf16[2,16384,1,128]{3,1,2,0:T(8,128)(2,1)} copy(bf16[2,16384,1,128]{1,3,2,0:T(8,128)(2,1)} %all-gather.2.cloned.1.call-done) | data formatting | bytes 16777216
  210.6 131.0 %while.20 = (s32[]{:T(128)}, f32[1,4,512]{2,1,0:T(4,128)S(1)}, f32[1,4,512]{2,1,0:T(4,128)S(1)}, f32[1,4,512,128]{3,2,1,0:T(8,128)S(1)}, s32[]{:T(128)}, /*index...) while((s32[]{:T(128)}, f32[1,4,512]{2,1,0:T(4,128)S(1)}, ...), condition=%wide.region_13.14_spmd.clone, body=%wide.region_7.13_spmd.clone.sunk | while | flops 549821440 | bytes 33448608 | solution.py:122
  210.7 0.6 slice.77
  214.1 8.9 %conditional.3 = ((f32[1,4,512]{2,1,0:T(4,128)S(1)}, f32[1,4,512]{2,1,0:T(4,128)S(1)}, f32[1,4,512,128]{3,2,1,0:T(8,128)S(1)})) conditional(s32[]{:T(128)} %convert_element_type.114, (f32[1,4,512]{2,1,0:T(4,128)S(1)}, f32[1,4,512]{2,1,0:T(4,128)S(1)}, f32[1,4,512,128]{3,2,1,0:T(8,128)S(1)}) %tuple.65, (s32[512]{0:T(512)S(1)}, s32[512]{0:T(512)S(1)}, ...), branch_computations={%region_9.9_spmd, %region_10.12_spmd} | conditional | flops 549722624 | bytes 33435770 | solution.py:115
  214.4 3.7 fusion.2
  218.2 3.8 fusion.14
  222.0 0.9 fusion.6
  223.1 0.6 slice.77
  226.5 8.8 %conditional.3 = ((f32[1,4,512]{2,1,0:T(4,128)S(1)}, f32[1,4,512]{2,1,0:T(4,128)S(1)}, f32[1,4,512,128]{3,2,1,0:T(8,128)S(1)})) conditional(s32[]{:T(128)} %convert_element_type.114, (f32[1,4,512]{2,1,0:T(4,128)S(1)}, f32[1,4,512]{2,1,0:T(4,128)S(1)}, f32[1,4,512,128]{3,2,1,0:T(8,128)S(1)}) %tuple.65, (s32[512]{0:T(512)S(1)}, s32[512]{0:T(512)S(1)}, ...), branch_computations={%region_9.9_spmd, %region_10.12_spmd} | conditional | flops 549722624 | bytes 33435770 | solution.py:115
  226.8 3.7 fusion.2
  230.6 3.8 fusion.14
  234.4 0.9 fusion.6
  342.1 6.6 %convolution_convert_fusion = bf16[512,4096]{1,0:T(8,128)(2,1)} fusion(bf16[512,512]{0,1:T(8,128)(2,1)S(1)} %bitcast.104, bf16[512,4096]{1,0:T(8,128)(2,1)} %param.16), kind=kOutput, calls=%fused_computation.30 | convolution fusion | flops 2149580800 | bytes 8912896 | tf_op jit(solution)/shard_map/dot_general | solution.py:130
  348.7 185.8 %reduce-scatter.2.cloned.1.call-done = bf16[512,512]{1,0:T(8,128)(2,1)} async-done(((bf16[512,4096]{1,0:T(8,128)(2,1)}), bf16[512,512]{1,0:T(8,128)(2,1)}) %reduce-scatter.2.cloned.1.call-update) | async-done | bytes 524304 | tf_op jit(solution)/shard_map/reduce_scatter | solution.py:131
  (265 shorter events, 38.9 us)
Async XLA Ops:
  6.5 120.4 %copy-start = (bf16[4096,128]{1,0:T(8,128)(2,1)S(1)}, bf16[4096,128]{1,0:T(8,128)(2,1)}, u32[]{:S(2)}) copy-start(bf16[4096,128]{1,0:T(8,128)(2,1)} %param.14) | copy-start | bytes 3145732
  28.7 4.7 copy-start.4
  28.7 95.4 %all-to-all-start = ((bf16[8,512,512]{2,1,0:T(8,128)(2,1)}), bf16[8,512,512]{2,1,0:T(8,128)(2,1)}, u32[]{:S(2)}, u32[]{:S(2)}) async-start(bf16[8,512,512]{2,1,0:T(8,128)(2,1)} %stack.6), calls=%async_computation | async-start | bytes 8388608 | tf_op jit(solution)/shard_map/all_to_all | solution.py:52
  33.4 165.2 %all-gather.2.cloned.1.call-start = ((), (), s32[]{:S(2)}) async-start(), calls=%async_computation.2 | async-start | bytes 8650752 | tf_op jit(solution)/shard_map/all_gather | solution.py:104
  126.9 1.6 copy-start.3
  131.4 403.2 %reduce-scatter.2.cloned.1.call-start = ((), (), s32[]{:S(2)}) async-start(), calls=%async_computation.3 | async-start | bytes 4718592 | tf_op jit(solution)/shard_map/reduce_scatter | solution.py:131
  218.2 3.8 copy-start.2
  230.6 3.8 copy-start.2
  342.1 192.4 %copy-start.1 = (bf16[4096,128]{1,0:T(8,128)(2,1)S(1)}, bf16[4096,128]{1,0:T(8,128)(2,1)}, u32[]{:S(2)}) copy-start(bf16[4096,128]{1,0:T(8,128)(2,1)} %param.14) | copy-start | bytes 3145732
Sparse Core Ops, SparseCore 0:
  131.5 67.0 all-gather.1
  348.8 185.6 reduce-scatter.1
